TPU v7x, 32 devices: a whole 2x2x4 slice. The times are simulated.
32 devices in a mesh: parts: 2 (over x), ctx: 16 (over z, y, core).
Axes of the slice: x: 2, y: 2, z: 4, core: 2. Of those that a mesh axis runs over, the one named last changes fastest.
Arguments:
- query_proj: bfloat16 [4096, 4096], P(('parts', 'ctx')), parts along dimension 0, may hold values from -6 to 6
- key_proj: bfloat16 [4096, 4096], P(('parts', 'ctx')), parts along dimension 0, may hold values from -6 to 6
- value_proj: bfloat16 [4096, 4096], P(('parts', 'ctx')), parts along dimension 0, may hold values from -6 to 6
- cotangent: bfloat16 [4096, 2048], P(('parts', 'ctx')), parts along dimension 0, may hold values from -6 to 6
- out_weight: bfloat16 [4096, 2048], P('ctx'), may hold values from -0.125 to 0.125
- filters: float32 [256, 2048], P('ctx'), may hold values from -1.2 to 1.2
Outputs:
- query_grad: float32 [4096, 4096], P(('parts', 'ctx')), parts along dimension 0
- key_grad: float32 [4096, 4096], P(('parts', 'ctx')), parts along dimension 0
- value_grad: float32 [4096, 4096], P(('parts', 'ctx')), parts along dimension 0
- filter_grad: float32 [512, 2048], P(('parts', 'ctx')), parts along dimension 0
There are 2 independent parts, one for each index of `parts`. A program takes and returns all parts, laid end to end along the dimension named above; an argument that names none is the same for every part. Nothing has to cross between parts.
All inputs are finite; a program needn't handle non-finite values.
Results may differ from a plain program's by a relative error of at most 0.005.
Values may be sent and summed in bfloat16 or wider, within the bound.
A program may use at most 192 MiB of HBM per device.

v0:
```python
import math

import jax
import jax.numpy as jnp
from jax import lax
from jax.sharding import PartitionSpec as P

inner_len = 128


def dft_pair(size_count):
    index_row = jnp.arange(size_count, dtype=jnp.int32)
    phase = (index_row[:, None] * index_row[None, :] % size_count).astype(jnp.float32) * (
        -2.0 * math.pi / size_count
    )
    return (jnp.cos(phase), jnp.sin(phase))


def twist(spectrum, sign):
    outer_len = spectrum.shape[1]
    total = outer_len * inner_len
    outer_index = jnp.arange(outer_len, dtype=jnp.int32)[:, None, None]
    inner_index = jnp.arange(inner_len, dtype=jnp.int32)[None, None, :]
    phase = (outer_index * inner_index % total).astype(jnp.float32) * (-2.0 * math.pi / total)
    tw_real = jnp.cos(phase)
    tw_imag = jnp.sin(phase) * sign
    real_part = spectrum[0] * tw_real - spectrum[1] * tw_imag
    imag_part = spectrum[0] * tw_imag + spectrum[1] * tw_real
    return jnp.stack([real_part, imag_part])


def last_matrix(sign):
    last_real, last_imag = dft_pair(inner_len)
    last_imag = last_imag * sign
    return jnp.stack([jnp.stack([last_real, -last_imag]), jnp.stack([last_imag, last_real])])


def apply_last(spectrum, sign):
    return jnp.einsum(
        "qzcn,pqkn->pzck", spectrum, last_matrix(sign), precision=lax.Precision.HIGHEST
    )


def forward_spectrum(signal):
    half_rows = signal.shape[0]
    outer_len = 2 * half_rows
    lead_real, lead_imag = dft_pair(outer_len)
    lead = jnp.stack([lead_real[:, :half_rows], lead_imag[:, :half_rows]])
    spectrum = jnp.einsum("pzn,ncm->pzcm", lead, signal, precision=lax.Precision.HIGHEST)
    return apply_last(twist(spectrum, 1.0), 1.0)


def inverse_spectrum(spectrum, want_imag):
    outer_len = spectrum.shape[1]
    half_rows = outer_len // 2
    spectrum = twist(apply_last(spectrum, -1.0), -1.0)
    lead_real, lead_imag = dft_pair(outer_len)
    lead_real = lead_real[:half_rows]
    lead_imag = lead_imag[:half_rows]
    scale = 1.0 / (outer_len * inner_len)
    if want_imag:
        lead = jnp.stack([jnp.stack([lead_real, lead_imag]), jnp.stack([-lead_imag, lead_real])])
    else:
        lead = jnp.stack([lead_real, lead_imag])[None]
    return jnp.einsum("qzcm,pqtz->ptcm", spectrum, lead * scale, precision=lax.Precision.HIGHEST)


def to_blocks(array):
    seq_len, chans = array.shape
    return (
        array.astype(jnp.float32).reshape(seq_len // inner_len, inner_len, chans).transpose(0, 2, 1)
    )


def from_blocks(array):
    half_rows, chans, unused = array.shape
    return array.transpose(0, 2, 1).reshape(half_rows * inner_len, chans)


def channel_work(mixed, gated, filters):
    seq_len, chans = mixed.shape
    group_count = filters.shape[0]
    group_size = chans // group_count
    half_rows = seq_len // inner_len
    outer_len = 2 * half_rows
    split_shape = (2, outer_len, group_count, group_size, inner_len)
    mix_spec = forward_spectrum(to_blocks(mixed)).reshape(split_shape)
    gate_spec = forward_spectrum(to_blocks(gated)).reshape(split_shape)
    filter_blocks = filters.reshape(group_count, half_rows, inner_len).transpose(1, 0, 2)
    filt_spec = forward_spectrum(filter_blocks)[:, :, :, None, :]
    filt_real, filt_imag = (filt_spec[0], filt_spec[1])
    mix_real, mix_imag = (mix_spec[0], mix_spec[1])
    gate_real, gate_imag = (gate_spec[0], gate_spec[1])
    conv_real = filt_real * mix_real - filt_imag * mix_imag
    conv_imag = filt_real * mix_imag + filt_imag * mix_real
    corr_real = filt_real * gate_real + filt_imag * gate_imag
    corr_imag = filt_real * gate_imag - filt_imag * gate_real
    combined = jnp.stack([conv_real - corr_imag, conv_imag + corr_real]).reshape(
        2, outer_len, chans, inner_len
    )
    both = inverse_spectrum(combined, True)
    conv_out = from_blocks(both[0])
    mixed_grad = from_blocks(both[1])
    lag_real = jnp.sum(mix_real * gate_real + mix_imag * gate_imag, axis=2)
    lag_imag = jnp.sum(mix_real * gate_imag - mix_imag * gate_real, axis=2)
    lag_out = inverse_spectrum(jnp.stack([lag_real, lag_imag]), False)[0]
    filter_grad = lag_out.transpose(1, 0, 2).reshape(group_count, seq_len) * (
        group_size * seq_len
    ) ** (-0.5)
    return (conv_out, mixed_grad, filter_grad)


def rounded_product(left, right):
    product = (left.astype(jnp.float32) * right.astype(jnp.float32)).astype(jnp.bfloat16)
    return lax.optimization_barrier(product)


def per_device(query_proj, key_proj, value_proj, cotangent, out_weight, filters):
    grad_rows = jnp.einsum(
        "tj,cj->tc",
        cotangent,
        lax.all_gather(out_weight, "ctx", axis=0, tiled=True),
        preferred_element_type=jnp.float32,
    ).astype(jnp.bfloat16)
    query_cols, key_cols, value_cols, grad_cols = (
        lax.all_to_all(query_proj, "ctx", split_axis=1, concat_axis=0, tiled=True),
        lax.all_to_all(key_proj, "ctx", split_axis=1, concat_axis=0, tiled=True),
        lax.all_to_all(value_proj, "ctx", split_axis=1, concat_axis=0, tiled=True),
        lax.all_to_all(grad_rows, "ctx", split_axis=1, concat_axis=0, tiled=True),
    )
    mixed_cols = rounded_product(key_cols, value_cols)
    gated_cols = rounded_product(query_cols, grad_cols)
    conv_out, mixed_grad, filter_grad = channel_work(mixed_cols, gated_cols, filters)
    query_grad_cols = grad_cols.astype(jnp.float32) * conv_out
    query_grad, key_grad, value_grad = (
        lax.all_to_all(query_grad_cols, "ctx", split_axis=0, concat_axis=1, tiled=True),
        lax.all_to_all(
            mixed_grad * value_cols.astype(jnp.float32),
            "ctx",
            split_axis=0,
            concat_axis=1,
            tiled=True,
        ),
        lax.all_to_all(
            mixed_grad * key_cols.astype(jnp.float32),
            "ctx",
            split_axis=0,
            concat_axis=1,
            tiled=True,
        ),
    )
    return (query_grad, key_grad, value_grad, filter_grad)


def solution(mesh):
    placed = (
        P(("parts", "ctx"), None),
        P(("parts", "ctx"), None),
        P(("parts", "ctx"), None),
        P(("parts", "ctx"), None),
        P("ctx", None),
        P("ctx", None),
    )
    return jax.shard_map(
        per_device,
        mesh=mesh,
        in_specs=placed,
        out_specs=(
            P(("parts", "ctx"), None),
            P(("parts", "ctx"), None),
            P(("parts", "ctx"), None),
            P(("parts", "ctx"), None),
        ),
        check_vma=False,
    )
```

profile of v0, /device:TPU:13, one launch (start us, length us, event | category | flops | bytes accessed | tf_op | source)
XLA Modules:
  0.0 509.7 jit_solution(12436188474592288112)
XLA Ops:
  7.9 2.3 copy.98
  10.2 6.7 %all-to-all-start.1 = ((bf16[128,16,256]{0,2,1:T(8,128)(2,1)}), bf16[128,16,256]{0,2,1:T(8,128)(2,1)S(1)}, u32[]{:S(2)}, u32[]{:S(2)}) async-start(bf16[128,16,256]{0,2,1:T(8,128)(2,1)} %bitcast.30), calls=%async_computation.1 | async-start | bytes 2097152 | tf_op jit(solution)/shard_map/all_to_all | solution.py:127
  16.9 1.3 copy.100
  18.2 49.8 %all-to-all-done.1 = bf16[128,16,256]{0,2,1:T(8,128)(2,1)S(1)} async-done(((bf16[128,16,256]{0,2,1:T(8,128)(2,1)}), bf16[128,16,256]{0,2,1:T(8,128)(2,1)S(1)}, u32[]{:S(2)}, u32[]{:S(2)}) %all-to-all-start.1) | async-done | bytes 1048608 | tf_op jit(solution)/shard_map/all_to_all | solution.py:127
  68.0 4.0 all-to-all-start.2
  71.9 2.3 copy.107
  74.2 46.1 %all-to-all-done.2 = bf16[128,16,256]{0,2,1:T(8,128)(2,1)S(1)} async-done(((bf16[128,16,256]{0,2,1:T(8,128)(2,1)}), bf16[128,16,256]{0,2,1:T(8,128)(2,1)S(1)}, u32[]{:S(2)}, u32[]{:S(2)}) %all-to-all-start.2) | async-done | bytes 1048608 | tf_op jit(solution)/shard_map/all_to_all | solution.py:128
  120.3 7.1 %all-to-all-start.3 = ((bf16[128,16,256]{0,2,1:T(8,128)(2,1)}), bf16[128,16,256]{0,2,1:T(8,128)(2,1)}, u32[]{:S(2)}, u32[]{:S(2)}) async-start(bf16[128,16,256]{0,2,1:T(8,128)(2,1)} %bitcast.223), calls=%async_computation.3 | async-start | bytes 2097152 | tf_op jit(solution)/shard_map/all_to_all | solution.py:126
  129.2 57.2 %all-gather.2.cloned.1.call-done = bf16[4096,2048]{1,0:T(8,128)(2,1)} async-done(((bf16[256,2048]{1,0:T(8,128)(2,1)}), bf16[4096,2048]{1,0:T(8,128)(2,1)}) %all-gather.2.cloned.1.call-update) | async-done | bytes 16777232 | tf_op jit(solution)/shard_map/all_gather | solution.py:122
  186.4 12.4 %convolution_convert_fusion = bf16[128,4096]{1,0:T(8,128)(2,1)} fusion(bf16[128,2048]{1,0:T(8,128)(2,1)S(1)} %copy-done, bf16[4096,2048]{1,0:T(8,128)(2,1)} %all-gather.2.cloned.1.call-done), kind=kOutput, calls=%fused_computation.13 | convolution fusion | flops 2148007936 | bytes 18350080 | tf_op jit(solution)/shard_map/tj,cj->tc/dot_general | solution.py:119
  198.8 2.3 copy.145
  201.0 10.4 %all-to-all-start = ((bf16[128,16,256]{0,2,1:T(8,128)(2,1)}), bf16[128,16,256]{0,2,1:T(8,128)(2,1)}, u32[]{:S(2)}, u32[]{:S(2)}) async-start(bf16[128,16,256]{0,2,1:T(8,128)(2,1)} %bitcast.222), calls=%async_computation | async-start | bytes 2097152 | tf_op jit(solution)/shard_map/all_to_all | solution.py:129
  212.9 2.3 mul.851
  215.2 5.7 %copy.104 = f32[1,32,256,128]{2,3,1,0:T(8,128)} copy(f32[1,32,256,128]{3,2,1,0:T(8,128)} %bitcast.214) | data formatting | bytes 8388608 | tf_op jit(solution)/shard_map/mul | solution.py:94
  221.1 2.3 mul.862
  223.4 5.6 %copy.106 = f32[1,32,256,128]{2,3,1,0:T(8,128)} copy(f32[1,32,256,128]{3,2,1,0:T(8,128)} %bitcast.215) | data formatting | bytes 8388608 | tf_op jit(solution)/shard_map/mul | solution.py:94
  229.1 1.2 fusion.19
  230.8 5.6 %fusion.26 = f32[2,32,256,128]{3,1,2,0:T(8,128)} fusion(bf16[16,128,256]{1,0,2:T(8,128)(2,1)S(1)} %bitcast.218, f32[1,32,16]{2,1,0:T(8,128)S(1)} %get-tuple-element.47, f32[1,32,16]{2,1,0:T(8,128)S(1)} %get-tuple-element.48), kind=kOutput, calls=%fused_computation.48 | convolution fusion | flops 402654208 | bytes 9441280 | tf_op jit(solution)/shard_map/pzn,ncm->pzcm/dot_general | solution.py:49
  236.4 2.8 fusion.22
  239.7 3.4 fusion.24
  243.1 6.2 %multiply_subtract_fusion.3 = (f32[1,32,256,128]{3,1,2,0:T(8,128)}, f32[1,32,256,128]{3,1,2,0:T(8,128)}, f32[1,32,256,128]{3,1,2,0:T(8,128)S(1)}, f32[1,32,256,128]{3,1,2,0:T(8,128)}) fusion(f32[2,32,256,128]{3,1,2,0:T(8,128)S(1)} %bitcast.212, f32[32,128]{1,0:T(8,128)S(1)} %get-tuple-element.49, f32[32,128]{1,0:T(8,128)S(1)} %get-tuple-element.50, ...), kind=kLoop, calls=%fused_computation.23 | loop fusion | flops 12582912 | bytes 33587200 | tf_op jit(solution)/shard_map/sub | solution.py:27
  249.4 4.5 pad_maximum_fusion
  253.9 12.6 %fusion.9 = f32[2,32,256,128]{2,3,1,0:T(8,128)S(1)} fusion(f32[2,32,256,128]{3,1,2,0:T(8,128)S(1)} %pad_maximum_fusion, f32[1,2,128,128]{3,2,1,0:T(8,128)S(1)} %copy-done.6, f32[1,2,128,128]{3,2,1,0:T(8,128)S(1)} %copy-done.8), kind=kOutput, calls=%fused_computation.24 | convolution fusion | flops 6442516480 | bytes 17039360 | tf_op jit(solution)/shard_map/qzcn,pqkn->pzck/dot_general | solution.py:39
  266.5 3.2 pad_maximum_fusion.1
  269.7 16.7 %fusion.12 = f32[2,32,256,128]{2,3,1,0:T(8,128)} fusion(f32[2,32,256,128]{3,1,2,0:T(8,128)S(1)} %pad_maximum_fusion.1, f32[1,2,128,128]{3,2,1,0:T(8,128)S(1)} %copy-done.6, f32[1,2,128,128]{3,2,1,0:T(8,128)S(1)} %copy-done.8), kind=kOutput, calls=%fused_computation.25 | convolution fusion | flops 6442516480 | bytes 17039360 | tf_op jit(solution)/shard_map/qzcn,pqkn->pzck/dot_general | solution.py:39
  286.4 10.2 %multiply_add_fusion = (f32[1,32,256,128]{2,3,1,0:T(8,128)}, f32[1,32,256,128]{2,3,1,0:T(8,128)}, f32[1,32,256,128]{2,3,1,0:T(8,128)}, f32[1,32,256,128]{2,3,1,0:T(8,128)}) fusion(f32[2,32,256,128]{2,3,1,0:T(8,128)} %fusion.12, f32[2,32,256,128]{2,3,1,0:T(8,128)S(1)} %fusion.9, f32[1,32,256,128]{2,3,1,0:T(8,128)} %copy.106, f32[1,32,256,128]{2,3,1,0:T(8,128)S(1)} %copy-done.2), kind=kLoop, calls=%fused_computation.15 | loop fusion | flops 20971520 | bytes 41943040 | tf_op jit(solution)/shard_map/add | solution.py:104
  296.7 7.8 %maximum_bitcast_fusion = f32[2,32,256,128,1]{2,3,1,0,4:T(8,128)} fusion(f32[1,32,256,128]{2,3,1,0:T(8,128)} %get-tuple-element.20, f32[1,32,256,128]{2,3,1,0:T(8,128)} %get-tuple-element.21), kind=kLoop, calls=%fused_computation.2 | loop fusion | flops 2097152 | bytes 16777216 | tf_op jit(solution)/shard_map/stack | solution.py:98
  304.4 10.3 %copy.139 = f32[2,32,256,128,1]{3,1,0,2,4:T(8,128)} copy(f32[2,32,256,128,1]{2,3,1,0,4:T(8,128)} %maximum_bitcast_fusion) | data formatting | bytes 16777216 | tf_op jit(solution)/shard_map/stack | solution.py:98
  314.7 12.5 %convolution_bitcast_fusion = f32[2,32,256,128]{3,1,2,0:T(8,128)S(1)} fusion(f32[2,32,256,128,1]{3,1,0,2,4:T(8,128)} %copy.139, f32[1,2,128,128]{3,2,1,0:T(8,128)S(1)} %copy-done.11, f32[1,2,128,128]{3,2,1,0:T(8,128)S(1)} %copy-done.9), kind=kOutput, calls=%fused_computation.26 | convolution fusion | flops 6442516480 | bytes 17039360 | tf_op jit(solution)/shard_map/qzcn,pqkn->pzck/dot_general | solution.py:39
  327.2 1.3 multiply_subtract_fusion.1
  328.6 5.0 fusion.15
  333.6 5.3 %fusion.18 = (f32[16,128,256]{1,0,2:T(8,128)}, f32[16,128,256]{1,0,2:T(8,128)}, f32[16,128,256]{1,0,2:T(8,128)S(1)}) fusion(f32[2,16,256,128]{3,1,2,0:T(8,128)S(1)} %fusion.15, bf16[128,16,256]{0,2,1:T(8,128)(2,1)S(1)} %all-to-all-done.1, bf16[128,16,256]{0,2,1:T(8,128)(2,1)S(1)} %copy-done.4, bf16[128,16,256]{0,2,1:T(8,128)(2,1)} %all-to-all-done), kind=kLoop, calls=%fused_computation.33 | loop fusion | flops 3145728 | bytes 13631488 | tf_op jit(solution)/shard_map/mul | solution.py:145
  338.9 2.0 copy.120
  340.9 6.1 %all-to-all-start.4 = ((f32[16,128,256]{1,2,0:T(8,128)}), f32[16,128,256]{1,2,0:T(8,128)S(1)}, u32[]{:S(2)}, u32[]{:S(2)}) async-start(f32[16,128,256]{1,2,0:T(8,128)} %copy.120), calls=%async_computation.4 | async-start | bytes 4194304 | tf_op jit(solution)/shard_map/all_to_all | solution.py:136
  347.0 3.6 copy.121
  350.6 43.8 %all-to-all-done.4 = f32[16,128,256]{1,2,0:T(8,128)S(1)} async-done(((f32[16,128,256]{1,2,0:T(8,128)}), f32[16,128,256]{1,2,0:T(8,128)S(1)}, u32[]{:S(2)}, u32[]{:S(2)}) %all-to-all-start.4) | async-done | bytes 2097184 | tf_op jit(solution)/shard_map/all_to_all | solution.py:136
  394.4 4.9 all-to-all-start.5
  399.3 3.7 copy.122
  403.0 43.9 %all-to-all-done.5 = f32[16,128,256]{1,2,0:T(8,128)} async-done(((f32[16,128,256]{1,2,0:T(8,128)}), f32[16,128,256]{1,2,0:T(8,128)}, u32[]{:S(2)}, u32[]{:S(2)}) %all-to-all-start.5) | async-done | bytes 2097184 | tf_op jit(solution)/shard_map/all_to_all | solution.py:137
  446.8 5.3 %all-to-all-start.6 = ((f32[16,128,256]{1,2,0:T(8,128)}), f32[16,128,256]{1,2,0:T(8,128)}, u32[]{:S(2)}, u32[]{:S(2)}) async-start(f32[16,128,256]{1,2,0:T(8,128)} %copy.122), calls=%async_computation.6 | async-start | bytes 4194304 | tf_op jit(solution)/shard_map/all_to_all | solution.py:144
  452.1 5.6 %copy.125 = f32[1,32,256,128]{3,2,1,0:T(8,128)} copy(f32[1,32,256,128]{2,3,1,0:T(8,128)} %get-tuple-element.19) | data formatting | bytes 8388608 | tf_op jit(solution)/shard_map/sub | solution.py:105
  457.7 2.9 reduce_sum.19
  460.7 5.6 %copy.123 = f32[1,32,256,128]{3,2,1,0:T(8,128)} copy(f32[1,32,256,128]{2,3,1,0:T(8,128)} %get-tuple-element.18) | data formatting | bytes 8388608 | tf_op jit(solution)/shard_map/add | solution.py:104
  466.3 2.9 reduce_sum.18
  471.2 1.8 copy.128
  473.0 2.9 copy.129
  475.9 23.6 %all-to-all-done.6 = f32[16,128,256]{1,2,0:T(8,128)} async-done(((f32[16,128,256]{1,2,0:T(8,128)}), f32[16,128,256]{1,2,0:T(8,128)}, u32[]{:S(2)}, u32[]{:S(2)}) %all-to-all-start.6) | async-done | bytes 2097184 | tf_op jit(solution)/shard_map/all_to_all | solution.py:144
  499.5 2.9 copy.130
  (75 shorter events, 7.3 us)
Async XLA Ops:
  7.2 179.2 %copy-start = (bf16[128,2048]{1,0:T(8,128)(2,1)S(1)}, bf16[128,2048]{1,0:T(8,128)(2,1)}, u32[]{:S(2)}) copy-start(bf16[128,2048]{1,0:T(8,128)(2,1)} %param.9) | copy-start | bytes 1572868
  7.2 9.7 %copy-start.13 = (bf16[128,4096]{1,0:T(8,128)(2,1)S(1)}, bf16[128,4096]{1,0:T(8,128)(2,1)}, u32[]{:S(2)}) copy-start(bf16[128,4096]{1,0:T(8,128)(2,1)} %param.8) | copy-start | bytes 3145732
  7.2 179.2 %all-gather.2.cloned.1.call-start = ((), (), s32[]{:S(2)}) async-start(), calls=%async_computation.7 | async-start | bytes 17825792 | tf_op jit(solution)/shard_map/all_gather | solution.py:122
  10.2 64.0 %copy-start.14 = (f32[16,2048]{1,0:T(8,128)S(1)}, f32[16,2048]{1,0:T(8,128)}, u32[]{:S(2)}) copy-start(f32[16,2048]{1,0:T(8,128)} %param.11) | copy-start | bytes 393220
  10.2 57.8 %all-to-all-start.1 = ((bf16[128,16,256]{0,2,1:T(8,128)(2,1)}), bf16[128,16,256]{0,2,1:T(8,128)(2,1)S(1)}, u32[]{:S(2)}, u32[]{:S(2)}) async-start(bf16[128,16,256]{0,2,1:T(8,128)(2,1)} %bitcast.30), calls=%async_computation.1 | async-start | bytes 2097152 | tf_op jit(solution)/shard_map/all_to_all | solution.py:127
  68.0 52.3 %all-to-all-start.2 = ((bf16[128,16,256]{0,2,1:T(8,128)(2,1)}), bf16[128,16,256]{0,2,1:T(8,128)(2,1)S(1)}, u32[]{:S(2)}, u32[]{:S(2)}) async-start(bf16[128,16,256]{0,2,1:T(8,128)(2,1)} %bitcast.224), calls=%async_computation.2 | async-start | bytes 2097152 | tf_op jit(solution)/shard_map/all_to_all | solution.py:128
  120.3 108.8 %copy-start.3 = (bf16[128,16,256]{0,2,1:T(8,128)(2,1)}, bf16[128,16,256]{0,2,1:T(8,128)(2,1)S(1)}, u32[]{:S(2)}) copy-start(bf16[128,16,256]{0,2,1:T(8,128)(2,1)S(1)} %all-to-all-done.2) | copy-start | bytes 3145732
  120.3 80.8 %all-to-all-start.3 = ((bf16[128,16,256]{0,2,1:T(8,128)(2,1)}), bf16[128,16,256]{0,2,1:T(8,128)(2,1)}, u32[]{:S(2)}, u32[]{:S(2)}) async-start(bf16[128,16,256]{0,2,1:T(8,128)(2,1)} %bitcast.223), calls=%async_computation.3 | async-start | bytes 2097152 | tf_op jit(solution)/shard_map/all_to_all | solution.py:126
  129.2 82.9 %copy-start.5 = (f32[1,2,128,128]{3,2,1,0:T(8,128)}, f32[1,2,128,128]{3,2,1,0:T(8,128)S(1)}, u32[]{:S(2)}) copy-start(f32[1,2,128,128]{3,2,1,0:T(8,128)S(1)} %get-tuple-element.38) | copy-start | bytes 393220
  129.2 82.9 %copy-start.7 = (f32[1,2,128,128]{3,2,1,0:T(8,128)}, f32[1,2,128,128]{3,2,1,0:T(8,128)S(1)}, u32[]{:S(2)}) copy-start(f32[1,2,128,128]{3,2,1,0:T(8,128)S(1)} %get-tuple-element.39) | copy-start | bytes 393220
  201.0 35.4 %all-to-all-start = ((bf16[128,16,256]{0,2,1:T(8,128)(2,1)}), bf16[128,16,256]{0,2,1:T(8,128)(2,1)}, u32[]{:S(2)}, u32[]{:S(2)}) async-start(bf16[128,16,256]{0,2,1:T(8,128)(2,1)} %bitcast.222), calls=%async_computation | async-start | bytes 2097152 | tf_op jit(solution)/shard_map/all_to_all | solution.py:129
  229.0 7.4 %copy-start.15 = (f32[1,16,32]{2,1,0:T(8,128)}, f32[1,16,32]{2,1,0:T(8,128)S(1)}, u32[]{:S(2)}) copy-start(f32[1,16,32]{2,1,0:T(8,128)S(1)} %get-tuple-element.43) | copy-start | bytes 6148
  229.1 7.4 %copy-start.17 = (f32[1,16,32]{2,1,0:T(8,128)}, f32[1,16,32]{2,1,0:T(8,128)S(1)}, u32[]{:S(2)}) copy-start(f32[1,16,32]{2,1,0:T(8,128)S(1)} %get-tuple-element.55) | copy-start | bytes 6148
  239.5 3.6 slice-start
  239.7 3.4 slice-start.1
  249.4 4.5 copy-start.6
  249.4 4.5 copy-start.8
  269.7 16.7 %copy-start.2 = (f32[1,32,256,128]{2,3,1,0:T(8,128)S(1)}, f32[1,32,256,128]{2,3,1,0:T(8,128)}, u32[]{:S(2)}) copy-start(f32[1,32,256,128]{2,3,1,0:T(8,128)} %copy.104) | copy-start | bytes 12582916
  304.4 10.3 %copy-start.9 = (f32[1,2,128,128]{3,2,1,0:T(8,128)S(1)}, f32[1,2,128,128]{3,2,1,0:T(8,128)}, u32[]{:S(2)}) copy-start(f32[1,2,128,128]{3,2,1,0:T(8,128)} %get-tuple-element.37) | copy-start | bytes 393220
  304.4 10.3 %copy-start.11 = (f32[1,2,128,128]{3,2,1,0:T(8,128)S(1)}, f32[1,2,128,128]{3,2,1,0:T(8,128)}, u32[]{:S(2)}) copy-start(f32[1,2,128,128]{3,2,1,0:T(8,128)} %get-tuple-element.40) | copy-start | bytes 393220
  328.6 5.0 copy-start.4
  340.9 53.5 %all-to-all-start.4 = ((f32[16,128,256]{1,2,0:T(8,128)}), f32[16,128,256]{1,2,0:T(8,128)S(1)}, u32[]{:S(2)}, u32[]{:S(2)}) async-start(f32[16,128,256]{1,2,0:T(8,128)} %copy.120), calls=%async_computation.4 | async-start | bytes 4194304 | tf_op jit(solution)/shard_map/all_to_all | solution.py:136
  394.4 52.4 %all-to-all-start.5 = ((f32[16,128,256]{1,2,0:T(8,128)}), f32[16,128,256]{1,2,0:T(8,128)}, u32[]{:S(2)}, u32[]{:S(2)}) async-start(f32[16,128,256]{1,2,0:T(8,128)} %copy.121), calls=%async_computation.5 | async-start | bytes 4194304 | tf_op jit(solution)/shard_map/all_to_all | solution.py:137
  446.8 52.7 %all-to-all-start.6 = ((f32[16,128,256]{1,2,0:T(8,128)}), f32[16,128,256]{1,2,0:T(8,128)}, u32[]{:S(2)}, u32[]{:S(2)}) async-start(f32[16,128,256]{1,2,0:T(8,128)} %copy.122), calls=%async_computation.6 | async-start | bytes 4194304 | tf_op jit(solution)/shard_map/all_to_all | solution.py:144
  466.3 3.0 copy-start.10
  466.3 3.0 copy-start.12
  466.3 3.8 copy-start.16
  466.3 3.8 copy-start.18
  473.0 29.4 %copy-start.1 = (bf16[128,2048]{1,0:T(8,128)(2,1)S(1)}, bf16[128,2048]{1,0:T(8,128)(2,1)}, u32[]{:S(2)}) copy-start(bf16[128,2048]{1,0:T(8,128)(2,1)} %param.9) | copy-start | bytes 1572868
Sparse Core Ops, SparseCore 0:
  10.2 176.1 all-gather.1
where the time goes:
time: 516 us; the launch traced here: 510 us
  waiting for transfers between devices  265 us (51%)
  matrix products  70.3 us (14%)
  local copies, waits for them, and re-layouts  64.6 us (13%)
  other arithmetic  50.4 us (10%)
  starting transfers between devices  44.4 us (9%)
  between operations  14.9 us (3%)
    all_gather x1, waiting for transfers between devices, per_device(): lax.all_gather(out_weight, 'ctx', axis=0, tiled=True)  57.2 us
    all_to_all x1, waiting for transfers between devices, per_device(): lax.all_to_all(key_proj, 'ctx', split_axis=1, concat_axis=0, tiled=True)  49.8 us
    all_to_all x1, waiting for transfers between devices, per_device(): lax.all_to_all(value_proj, 'ctx', split_axis=1, concat_axis=0, tiled=True)  46.1 us
    all_to_all x1, waiting for transfers between devices, per_device(): lax.all_to_all(mixed_grad * value_cols.astype(jnp.float32), 'ctx', split_...  43.9 us
    all_to_all x1, waiting for transfers between devices, per_device(): lax.all_to_all(query_grad_cols, 'ctx', split_axis=0, concat_axis=1, tiled...  43.8 us
    dot_general x5, matrix products, apply_last(): jnp.einsum('qzcn,pqkn->pzck', spectrum, last_matrix(sign), precision=lax....  43 us
    all_to_all x1, waiting for transfers between devices, per_device(): lax.all_to_all(mixed_grad * key_cols.astype(jnp.float32), 'ctx', split_ax...  23.6 us
    mul x7, local copies, waits for them, and re-layouts, channel_work(): conv_real = filt_real * mix_real - filt_imag * mix_imag  16.2 us
  transfers between devices with their start and end apart: 8, of which 6 were waited for; matrix products, arithmetic and copies ran while one was open for 15% of the time, Pallas kernels for 0%

commit v1 on v0

--- a/solution.py
+++ b/solution.py
@@ -3,6 +3,8 @@
 import jax
 import jax.numpy as jnp
 from jax import lax
+from jax.experimental import pallas as pl
+from jax.experimental.pallas import tpu as pltpu
 from jax.sharding import PartitionSpec as P
 
 inner_len = 128
@@ -152,6 +154,199 @@
     return (query_grad, key_grad, value_grad, filter_grad)
 
 
+blocks = 16
+lane = 128
+group_size = 16
+
+
+def stack_pairs(tile):
+    pairs = tile.reshape(8, 2, group_size, lane)
+    return jnp.concatenate(
+        [pairs[:, 0].reshape(lane, lane), pairs[:, 1].reshape(lane, lane)], axis=1
+    )
+
+
+def shift_down(rows, count):
+    if count == 0:
+        return rows
+    return jnp.concatenate([jnp.zeros((count, rows.shape[1]), rows.dtype), rows[:-count]], axis=0)
+
+
+def shift_up(rows, count):
+    if count == 0:
+        return rows
+    return jnp.concatenate([rows[count:], jnp.zeros((count, rows.shape[1]), rows.dtype)], axis=0)
+
+
+def toeplitz(filter_row):
+    seq_len = filter_row.shape[1]
+    wide = jnp.broadcast_to(filter_row, (lane, seq_len))
+    rolled = pltpu.roll(wide, 0, 1, stride=1, stride_axis=0)
+    row_at = lax.broadcasted_iota(jnp.int32, (lane, lane), 0)
+    lane_at = lax.broadcasted_iota(jnp.int32, (lane, lane), 1)
+    first = jnp.where(lane_at >= row_at, rolled[:, :lane], 0.0)
+    top = jnp.concatenate([first, rolled[:, lane:]], axis=1).astype(jnp.bfloat16)
+    low = jnp.concatenate([jnp.zeros((lane, lane), jnp.bfloat16), top[:, :-lane]], axis=1)
+    return jnp.concatenate([top, low], axis=0)
+
+
+nt_dims = (((1,), (1,)), ((), ()))
+
+
+def grad_block(pair, weight_ref, cot_ref, grad_ref):
+    cot = cot_ref[pl.ds(2 * pair, 2)].reshape(2 * lane, cot_ref.shape[2])
+    grad = lax.dot_general(weight_ref[...], cot, nt_dims, preferred_element_type=jnp.float32)
+    grad = grad.astype(jnp.bfloat16)
+    grad_ref[2 * pair] = grad[:, :lane]
+    grad_ref[2 * pair + 1] = grad[:, lane:]
+
+
+def store_pairs(out_ref, rows, value):
+    value = value.reshape(8, group_size, 2 * lane)
+    for index in range(8):
+        out_ref[2 * index, rows, :] = value[index, :, :lane].astype(out_ref.dtype)
+        out_ref[2 * index + 1, rows, :] = value[index, :, lane:].astype(out_ref.dtype)
+
+
+def group_rows(group):
+    return pl.ds(pl.multiple_of(group * group_size, group_size), group_size)
+
+
+def conv_group(group, mixed_ref, filt_ref, toep_ref, conv_ref):
+    rows = group_rows(group)
+    toep = toeplitz(filt_ref[pl.ds(group, 1), :])
+    toep_ref[group] = toep
+    mixed = stack_pairs(mixed_ref[:, rows, :])
+    left = jnp.concatenate([shift_down(mixed, group_size * step) for step in range(8)], axis=1)
+    right = jnp.concatenate(
+        [toep[:, 2 * lane * step : 2 * lane * (step + 1)] for step in range(8)], axis=0
+    )
+    store_pairs(conv_ref, rows, jnp.dot(left, right, preferred_element_type=jnp.float32))
+
+
+def query_group(group, conv_ref, grad_ref, out_ref):
+    rows = group_rows(group)
+    out_ref[:, rows, :] = (
+        conv_ref[:, rows, :] * grad_ref[:, rows, :].astype(jnp.float32)
+    ).astype(out_ref.dtype)
+
+
+def gated_of(rows, query_ref, grad_ref):
+    return (
+        query_ref[:, rows, :].astype(jnp.float32) * grad_ref[:, rows, :].astype(jnp.float32)
+    ).astype(jnp.bfloat16)
+
+
+def corr_group(group, query_ref, grad_ref, toep_ref, out_ref):
+    rows = group_rows(group)
+    gated = stack_pairs(gated_of(rows, query_ref, grad_ref))
+    left = jnp.concatenate([shift_up(gated, group_size * step) for step in range(8)], axis=1)
+    store_pairs(
+        out_ref,
+        rows,
+        lax.dot_general(left, toep_ref[group], nt_dims, preferred_element_type=jnp.float32),
+    )
+
+
+def lag_group(group, mixed_ref, query_ref, grad_ref, lag_ref):
+    rows = group_rows(group)
+    gated = gated_of(rows, query_ref, grad_ref).reshape(2 * lane, lane)
+    right = jnp.concatenate([shift_up(gated, group_size * step) for step in range(blocks)], axis=1)
+    row_at = lax.broadcasted_iota(jnp.int32, (lane, lane), 0)
+    lane_at = lax.broadcasted_iota(jnp.int32, (lane, lane), 1)
+    flip = jnp.where(row_at + lane_at == lane - 1, 1.0, 0.0).astype(jnp.bfloat16)
+    mixed = mixed_ref[:, rows, :].reshape(2 * lane, lane)
+    left = lax.dot_general(flip, mixed, nt_dims, preferred_element_type=jnp.float32)
+    cross = jnp.dot(left.astype(jnp.bfloat16), right, preferred_element_type=jnp.float32)
+    cross = jnp.concatenate([cross, jnp.zeros((lane, lane), jnp.float32)], axis=1)
+    rolled = pltpu.roll(cross, 0, 1, stride=1, stride_axis=0)
+    lag_ref[pl.ds(group, 1), :] = jnp.sum(rolled, axis=0, keepdims=True)
+
+
+def finish_lag(lag_ref, out_ref):
+    seq_len = out_ref.shape[1]
+    scale = (group_size * seq_len) ** -0.5
+    rolled = pltpu.roll(lag_ref[...], seq_len + 1, 1)
+    out_ref[...] = rolled[:, :seq_len] * scale
+
+
+def channel_kernel(
+    mixed_ref, query_ref, cot_ref, weight_ref, filt_ref,
+    qgrad_ref, mgrad_ref, fgrad_ref,
+    grad_ref, conv_ref, toep_ref, lag_ref,
+):
+    @pl.loop(0, 8)
+    def _(pair):
+        grad_block(pair, weight_ref, cot_ref, grad_ref)
+
+    @pl.loop(0, blocks)
+    def _(group):
+        conv_group(group, mixed_ref, filt_ref, toep_ref, conv_ref)
+        query_group(group, conv_ref, grad_ref, qgrad_ref)
+        corr_group(group, query_ref, grad_ref, toep_ref, mgrad_ref)
+        lag_group(group, mixed_ref, query_ref, grad_ref, lag_ref)
+
+    finish_lag(lag_ref, fgrad_ref)
+
+
+def final_kernel(qgrad_ref, mgrad_ref, key_ref, value_ref, query_out, key_out, value_out):
+    query_out[...] = qgrad_ref[...].astype(jnp.float32).T
+    mgrad = mgrad_ref[...].astype(jnp.float32).T
+    key_out[...] = mgrad * value_ref[...].astype(jnp.float32)
+    value_out[...] = mgrad * key_ref[...].astype(jnp.float32)
+
+
+def finish(qgrad, mgrad, key_proj, value_proj):
+    chans = key_proj.shape[1]
+    wide = chans // 4
+    return pl.pallas_call(
+        final_kernel,
+        grid=(4,),
+        in_specs=[pl.BlockSpec((wide, lane), lambda i: (i, 0))] * 2
+        + [pl.BlockSpec((lane, wide), lambda i: (0, i))] * 2,
+        out_specs=[pl.BlockSpec((lane, wide), lambda i: (0, i))] * 3,
+        out_shape=[jax.ShapeDtypeStruct(key_proj.shape, jnp.float32)] * 3,
+        compiler_params=pltpu.CompilerParams(vmem_limit_bytes=32 * 1024 * 1024),
+        cost_estimate=pl.CostEstimate(flops=1 << 20, bytes_accessed=10 << 20, transcendentals=0),
+    )(qgrad.reshape(chans, lane), mgrad.reshape(chans, lane), key_proj, value_proj)
+
+
+def direct_device(query_proj, key_proj, value_proj, cotangent, out_weight, filters):
+    own = out_weight.shape[0]
+    features = cotangent.shape[1]
+    seq_len = filters.shape[1]
+    tile_shape = (blocks, own, lane)
+    mixed = rounded_product(key_proj, value_proj).T.reshape(tile_shape)
+    query = query_proj.T.reshape(tile_shape)
+    mixed_cols = lax.all_to_all(mixed, "ctx", split_axis=0, concat_axis=0, tiled=True)
+    query_cols = lax.all_to_all(query, "ctx", split_axis=0, concat_axis=0, tiled=True)
+    cot_all = lax.all_gather(cotangent, "ctx", axis=0, tiled=True).reshape(blocks, lane, features)
+    vmem = pl.BlockSpec(memory_space=pltpu.VMEM)
+    qgrad, mgrad, filter_grad = pl.pallas_call(
+        channel_kernel,
+        in_specs=[vmem] * 5,
+        out_specs=[vmem] * 3,
+        out_shape=[
+            jax.ShapeDtypeStruct(tile_shape, jnp.bfloat16),
+            jax.ShapeDtypeStruct(tile_shape, jnp.bfloat16),
+            jax.ShapeDtypeStruct(filters.shape, jnp.float32),
+        ],
+        scratch_shapes=[
+            pltpu.VMEM(tile_shape, jnp.bfloat16),
+            pltpu.VMEM(tile_shape, jnp.float32),
+            pltpu.VMEM((blocks, 2 * lane, seq_len), jnp.bfloat16),
+            pltpu.VMEM((filters.shape[0], seq_len + lane), jnp.float32),
+        ],
+        compiler_params=pltpu.CompilerParams(vmem_limit_bytes=52 * 1024 * 1024),
+        cost_estimate=pl.CostEstimate(
+            flops=8 << 30, bytes_accessed=16 << 20, transcendentals=0
+        ),
+    )(mixed_cols, query_cols, cot_all, out_weight, filters)
+    qgrad = lax.all_to_all(qgrad, "ctx", split_axis=0, concat_axis=0, tiled=True)
+    mgrad = lax.all_to_all(mgrad, "ctx", split_axis=0, concat_axis=0, tiled=True)
+    return (*finish(qgrad, mgrad, key_proj, value_proj), filter_grad)
+
+
 def solution(mesh):
     placed = (
         P(("parts", "ctx"), None),
@@ -161,8 +356,9 @@
         P("ctx", None),
         P("ctx", None),
     )
+    work = direct_device if mesh.shape["ctx"] == blocks else per_device
     return jax.shard_map(
-        per_device,
+        work,
         mesh=mesh,
         in_specs=placed,
         out_specs=(

time: 516 us -> 221 us (0.43)
  the two profiles are of different devices: /device:TPU:13 before, /device:TPU:0 now
where the time goes in v1:
time: 221 us; the launch traced here: 220 us
  blocking collectives  114 us (52%)
  waiting for transfers between devices  50.9 us (23%)
  Pallas kernels  29.1 us (13%)
  between operations  14.1 us (6%)
  starting transfers between devices  7.47 us (3%)
  local copies, waits for them, and re-layouts  3.74 us (2%)
    all_to_all x1, blocking collectives, direct_device(): lax.all_to_all(mixed, 'ctx', split_axis=0, concat_axis=0, tiled=True)  56.4 us
    all_to_all x1, waiting for transfers between devices, direct_device(): lax.all_to_all(query, 'ctx', split_axis=0, concat_axis=0, tiled=True)  35.4 us
    all_to_all x1, blocking collectives, direct_device(): lax.all_to_all(mgrad, 'ctx', split_axis=0, concat_axis=0, tiled=True)  29.6 us
    all_to_all x1, blocking collectives, direct_device(): lax.all_to_all(qgrad, 'ctx', split_axis=0, concat_axis=0, tiled=True)  28.4 us
    pallas_call x1, Pallas kernels, direct_device(): pl.pallas_call(channel_kernel, in_specs=[vmem] * 5, out_specs=[vmem] * 3,...  25.9 us
    all_gather x1, waiting for transfers between devices, direct_device(): lax.all_gather(cotangent, 'ctx', axis=0, tiled=True)  14.8 us
    all_to_all x1, starting transfers between devices, direct_device(): lax.all_to_all(query, 'ctx', split_axis=0, concat_axis=0, tiled=True)  7.44 us
  transfers between devices with their start and end apart: 2, of which 2 were waited for; matrix products, arithmetic and copies ran while one was open for 2% of the time, Pallas kernels for 0%

profile of v1, /device:TPU:0, one launch (start us, length us, event | category | flops | bytes accessed | tf_op | source)
XLA Modules:
  0.0 219.9 jit_solution(17861230912564908898)
XLA Ops:
  7.2 0.0 all-gather.2.cloned.1.call-start
  7.2 0.7 all-gather.2.cloned.1.call-update
  7.9 0.0 copy-start
  7.9 0.0 copy-start.1
  7.9 2.4 %copy.11 = bf16[4096,128]{1,0:T(8,128)(2,1)} copy(bf16[4096,128]{0,1:T(8,128)(2,1)} %bitcast.11) | data formatting | bytes 2097152 | tf_op jit(solution)/shard_map/transpose | solution.py:320
  10.3 7.4 %all-to-all-start.1 = ((bf16[16,256,128]{2,1,0:T(8,128)(2,1)}), bf16[16,256,128]{2,1,0:T(8,128)(2,1)}, u32[]{:S(2)}, u32[]{:S(2)}) async-start(bf16[16,256,128]{2,1,0:T(8,128)(2,1)} %bitcast.3), calls=%async_computation.1 | async-start | bytes 2097152 | tf_op jit(solution)/shard_map/all_to_all | solution.py:322
  17.8 0.0 copy-done
  17.8 0.0 copy-done.1
  17.8 0.2 multiply_convert_fusion
  18.0 0.0 copy-start.2
  18.1 1.3 copy.10
  19.4 35.4 %all-to-all-done.1.query_ref = bf16[16,256,128]{2,1,0:T(8,128)(2,1)} async-done(((bf16[16,256,128]{2,1,0:T(8,128)(2,1)}), bf16[16,256,128]{2,1,0:T(8,128)(2,1)}, u32[]{:S(2)}, u32[]{:S(2)}) %all-to-all-start.1) | async-done | bytes 1048608 | tf_op jit(solution)/shard_map/all_to_all | solution.py:322
  54.8 56.4 %all_to_all.20.mixed_ref = bf16[16,256,128]{2,1,0:T(8,128)(2,1)} all-to-all(bf16[16,256,128]{2,1,0:T(8,128)(2,1)} %bitcast.10), channel_id=1, replica_groups=mesh['parts'=2,'ctx'=16] {'ctx'}, dimensions={0} | all-to-all | bytes 2097152 | tf_op jit(solution)/shard_map/all_to_all | solution.py:321
  111.1 14.8 %all-gather.2.cloned.1.call-done = bf16[2048,2048]{1,0:T(8,128)(2,1)} async-done(((bf16[128,2048]{1,0:T(8,128)(2,1)}), bf16[2048,2048]{1,0:T(8,128)(2,1)}) %all-gather.2.cloned.1.call-update) | async-done | bytes 8388624 | tf_op jit(solution)/shard_map/all_gather | solution.py:323
  125.9 0.0 copy-done.2
  125.9 25.9 %shard_map.93 = (bf16[16,256,128]{2,1,0:T(8,128)(2,1)S(1)}, bf16[16,256,128]{2,1,0:T(8,128)(2,1)}, f32[16,2048]{1,0:T(8,128)}) custom-call(bf16[16,256,128]{2,1,0:T(8,128)(2,1)} %all_to_all.20.mixed_ref, bf16[16,256,128]{2,1,0:T(8,128)(2,1)} %all-to-all-done.1.query_ref, bf16[16,128,2048]{2,1,0:T(8,128)(2,1)} %bitcast.12, bf16[256,2048]{1,0:T(8,128)(2,1)} %weight_ref.1, ...), custom_call_target="tpu_custom_call" | custom-call | flops 8589934592 | bytes 16777216 | tf_op jit(solution)/shard_map/pallas_call | solution.py:325
  151.8 0.0 copy-start.3
  151.8 28.4 %all_to_all.21 = bf16[16,256,128]{2,1,0:T(8,128)(2,1)S(1)} all-to-all(bf16[16,256,128]{2,1,0:T(8,128)(2,1)S(1)} %get-tuple-element.10), channel_id=1, replica_groups=mesh['parts'=2,'ctx'=16] {'ctx'}, dimensions={0} | all-to-all | bytes 2097152 | tf_op jit(solution)/shard_map/all_to_all | solution.py:345
  180.3 0.0 copy-done.3
  180.3 29.6 %all_to_all.22 = bf16[16,256,128]{2,1,0:T(8,128)(2,1)S(1)} all-to-all(bf16[16,256,128]{2,1,0:T(8,128)(2,1)S(1)} %copy-done.3), channel_id=1, replica_groups=mesh['parts'=2,'ctx'=16] {'ctx'}, dimensions={0} | all-to-all | bytes 2097152 | tf_op jit(solution)/shard_map/all_to_all | solution.py:346
  209.9 3.2 %shard_map.94 = (f32[128,4096]{1,0:T(8,128)}, f32[128,4096]{1,0:T(8,128)}, f32[128,4096]{1,0:T(8,128)}) custom-call(bf16[4096,128]{1,0:T(8,128)(2,1)S(1)} %bitcast.7, bf16[4096,128]{1,0:T(8,128)(2,1)S(1)} %bitcast.8, bf16[128,4096]{1,0:T(8,128)(2,1)S(1)} %copy-done.1, bf16[128,4096]{1,0:T(8,128)(2,1)S(1)} %copy-done), custom_call_target="tpu_custom_call" | custom-call | flops 1048576 | bytes 10485760 | tf_op jit(solution)/shard_map/pallas_call | solution.py:302
Async XLA Ops:
  7.2 118.8 %all-gather.2.cloned.1.call-start = ((), (), s32[]{:S(2)}) async-start(), calls=%async_computation.4 | async-start | bytes 8912896 | tf_op jit(solution)/shard_map/all_gather | solution.py:323
  7.9 9.9 %copy-start = (bf16[128,4096]{1,0:T(8,128)(2,1)S(1)}, bf16[128,4096]{1,0:T(8,128)(2,1)}, u32[]{:S(2)}) copy-start(bf16[128,4096]{1,0:T(8,128)(2,1)} %value_ref.1) | copy-start | bytes 3145732
  7.9 9.9 %copy-start.1 = (bf16[128,4096]{1,0:T(8,128)(2,1)S(1)}, bf16[128,4096]{1,0:T(8,128)(2,1)}, u32[]{:S(2)}) copy-start(bf16[128,4096]{1,0:T(8,128)(2,1)} %key_ref.1) | copy-start | bytes 3145732
  10.3 44.4 %all-to-all-start.1 = ((bf16[16,256,128]{2,1,0:T(8,128)(2,1)}), bf16[16,256,128]{2,1,0:T(8,128)(2,1)}, u32[]{:S(2)}, u32[]{:S(2)}) async-start(bf16[16,256,128]{2,1,0:T(8,128)(2,1)} %bitcast.3), calls=%async_computation.1 | async-start | bytes 2097152 | tf_op jit(solution)/shard_map/all_to_all | solution.py:322
  18.0 107.9 %copy-start.2 = (f32[16,2048]{1,0:T(8,128)S(1)}, f32[16,2048]{1,0:T(8,128)}, u32[]{:S(2)}) copy-start(f32[16,2048]{1,0:T(8,128)} %filt_ref.1) | copy-start | bytes 393220
  151.8 28.5 %copy-start.3 = (bf16[16,256,128]{2,1,0:T(8,128)(2,1)S(1)}, bf16[16,256,128]{2,1,0:T(8,128)(2,1)}, u32[]{:S(2)}) copy-start(bf16[16,256,128]{2,1,0:T(8,128)(2,1)} %get-tuple-element.11) | copy-start | bytes 3145732
Sparse Core Ops, SparseCore 0:
  10.2 115.7 all-gather.1

commit v2 on v1

--- a/solution.py
+++ b/solution.py
@@ -212,10 +212,9 @@
     return pl.ds(pl.multiple_of(group * group_size, group_size), group_size)
 
 
-def conv_group(group, mixed_ref, filt_ref, toep_ref, conv_ref):
+def conv_group(group, mixed_ref, toep_ref, conv_ref):
     rows = group_rows(group)
-    toep = toeplitz(filt_ref[pl.ds(group, 1), :])
-    toep_ref[group] = toep
+    toep = toep_ref[group]
     mixed = stack_pairs(mixed_ref[:, rows, :])
     left = jnp.concatenate([shift_down(mixed, group_size * step) for step in range(8)], axis=1)
     right = jnp.concatenate(
@@ -270,23 +269,201 @@
     out_ref[...] = rolled[:, :seq_len] * scale
 
 
-def channel_kernel(
+def remote(src, dst, send, recv, peer):
+    return pltpu.make_async_remote_copy(
+        src_ref=src,
+        dst_ref=dst,
+        send_sem=send,
+        recv_sem=recv,
+        device_id={"ctx": peer},
+        device_id_type=pl.DeviceIdType.MESH,
+    )
+
+
+def slice_kernel(
     mixed_ref, query_ref, cot_ref, weight_ref, filt_ref,
-    qgrad_ref, mgrad_ref, fgrad_ref,
-    grad_ref, conv_ref, toep_ref, lag_ref,
+    qback_ref, mback_ref, fgrad_ref,
+    mixed_in, query_in, cot_in, qgrad_ref, mgrad_ref, grad_ref, conv_ref, toep_ref, lag_ref,
+    cot_send, cot_recv, mixed_send, mixed_recv, query_send, query_recv,
+    qback_send, qback_recv, mback_send, mback_recv, local_sem,
 ):
-    @pl.loop(0, 8)
-    def _(pair):
-        grad_block(pair, weight_ref, cot_ref, grad_ref)
+    me = lax.axis_index("ctx")
+    place_z, place_y, place_core = me // 4, (me // 2) % 2, me % 2
+    y_peer = me + 2 - 4 * place_y
+    core_peer = me + 1 - 2 * place_core
+
+    def peer_of(step):
+        return (me + step) % blocks
+
+    barrier = pltpu.get_barrier_semaphore()
+
+    @pl.loop(1, blocks)
+    def _(step):
+        pl.semaphore_signal(
+            barrier, inc=1, device_id={"ctx": peer_of(step)}, device_id_type=pl.DeviceIdType.MESH
+        )
+
+    pl.semaphore_wait(barrier, blocks - 1)
+
+    def cot_copy(src, block, way, peer):
+        return remote(src, cot_in.at[block], cot_send.at[way, block], cot_recv.at[block], peer)
+
+    def forward(src, block, ways, act):
+        if "u" in ways:
+            @pl.when(place_z < 3)
+            def _():
+                act(cot_copy(src, block, 0, me + 4))
+        if "d" in ways:
+            @pl.when(place_z > 0)
+            def _():
+                act(cot_copy(src, block, 1, me - 4))
+        if "y" in ways:
+            act(cot_copy(src, block, 2, y_peer))
+        if "c" in ways:
+            act(cot_copy(src, block, 3, core_peer))
+
+    def arrived(block):
+        cot_copy(cot_in.at[block], block, 3, core_peer).wait_recv()
+
+    def begin(copy):
+        copy.start()
+
+    def sent(copy):
+        copy.wait_send()
+
+    def relay_z(hop, act, wait):
+        @pl.when(place_z >= hop)
+        def _():
+            block = me - 4 * hop
+            if wait:
+                arrived(block)
+            forward(cot_in.at[block], block, "uyc", act)
+
+        @pl.when(place_z + hop <= 3)
+        def _():
+            block = me + 4 * hop
+            if wait:
+                arrived(block)
+            forward(cot_in.at[block], block, "dyc", act)
+
+    def relay_y(hop, act, wait):
+        def one(block):
+            if wait:
+                arrived(block)
+            forward(cot_in.at[block], block, "c", act)
+
+        if hop == 0:
+            one(y_peer)
+        else:
+            @pl.when(place_z >= hop)
+            def _():
+                one(y_peer - 4 * hop)
+
+            @pl.when(place_z + hop <= 3)
+            def _():
+                one(y_peer + 4 * hop)
+
+    def start_all(src, dst, send, recv, local, rows):
+        pltpu.make_async_copy(src.at[me, rows], dst.at[me, rows], local).start()
+
+        @pl.loop(1, blocks)
+        def _(step):
+            peer = peer_of(step)
+            remote(src.at[peer, rows], dst.at[me, rows], send.at[peer], recv.at[me], peer).start()
+
+    def wait_arrivals(src, dst, send, recv, local, rows):
+        pltpu.make_async_copy(src.at[me, rows], dst.at[me, rows], local).wait()
+
+        @pl.loop(1, blocks)
+        def _(step):
+            peer = peer_of(step)
+            remote(
+                src.at[peer, rows], dst.at[peer, rows], send.at[peer], recv.at[peer], peer
+            ).wait_recv()
+
+    def wait_sends(src, dst, send, recv, local, rows):
+        @pl.loop(1, blocks)
+        def _(step):
+            peer = peer_of(step)
+            remote(
+                src.at[peer, rows], dst.at[me, rows], send.at[peer], recv.at[me], peer
+            ).wait_send()
+
+    every = pl.ds(0, mixed_in.shape[1])
+    mixed_trip = (mixed_ref, mixed_in, mixed_send, mixed_recv, local_sem.at[0], every)
+    query_trip = (query_ref, query_in, query_send, query_recv, local_sem.at[1], every)
+    qback_trip = (qgrad_ref, qback_ref, qback_send, qback_recv, local_sem.at[2], every)
+    halves = 2
+    half_rows = mixed_in.shape[1] // halves
+    mback_trips = [
+        (
+            mgrad_ref, mback_ref, mback_send.at[half], mback_recv.at[half],
+            local_sem.at[4 + half], pl.ds(half * half_rows, half_rows),
+        )
+        for half in range(halves)
+    ]
+
+    forward(cot_ref, me, "udyc", begin)
+    own_cot = pltpu.make_async_copy(cot_ref, cot_in.at[me], local_sem.at[3])
+    own_cot.start()
+    start_all(*mixed_trip)
 
     @pl.loop(0, blocks)
     def _(group):
-        conv_group(group, mixed_ref, filt_ref, toep_ref, conv_ref)
+        toep_ref[group] = toeplitz(filt_ref[pl.ds(group, 1), :])
+
+    relay_z(1, begin, True)
+    relay_y(0, begin, True)
+    relay_z(2, begin, True)
+    relay_y(1, begin, True)
+    start_all(*query_trip)
+    relay_z(3, begin, True)
+    wait_arrivals(*mixed_trip)
+
+    @pl.loop(0, blocks)
+    def _(group):
+        conv_group(group, mixed_in, toep_ref, conv_ref)
+
+    relay_y(2, begin, True)
+    relay_y(3, begin, True)
+    own_cot.wait()
+
+    @pl.loop(0, blocks // 2)
+    def _(pair):
+        arrived(2 * pair + 1 - place_core)
+
+    @pl.loop(0, blocks // 2)
+    def _(pair):
+        grad_block(pair, weight_ref, cot_in, grad_ref)
+
+    @pl.loop(0, blocks)
+    def _(group):
         query_group(group, conv_ref, grad_ref, qgrad_ref)
-        corr_group(group, query_ref, grad_ref, toep_ref, mgrad_ref)
-        lag_group(group, mixed_ref, query_ref, grad_ref, lag_ref)
+
+    start_all(*qback_trip)
+    wait_arrivals(*query_trip)
+    for half in range(halves):
+        @pl.loop(half * blocks // halves, (half + 1) * blocks // halves)
+        def _(group):
+            corr_group(group, query_in, grad_ref, toep_ref, mgrad_ref)
+
+        start_all(*mback_trips[half])
+
+    @pl.loop(0, blocks)
+    def _(group):
+        lag_group(group, mixed_in, query_in, grad_ref, lag_ref)
 
     finish_lag(lag_ref, fgrad_ref)
+
+    forward(cot_ref, me, "udyc", sent)
+    for hop in (1, 2, 3):
+        relay_z(hop, sent, False)
+    for hop in (0, 1, 2, 3):
+        relay_y(hop, sent, False)
+    for trip in [mixed_trip, query_trip, qback_trip] + mback_trips:
+        wait_sends(*trip)
+    for trip in [qback_trip] + mback_trips:
+        wait_arrivals(*trip)
 
 
 def final_kernel(qgrad_ref, mgrad_ref, key_ref, value_ref, query_out, key_out, value_out):
@@ -318,32 +495,48 @@
     tile_shape = (blocks, own, lane)
     mixed = rounded_product(key_proj, value_proj).T.reshape(tile_shape)
     query = query_proj.T.reshape(tile_shape)
-    mixed_cols = lax.all_to_all(mixed, "ctx", split_axis=0, concat_axis=0, tiled=True)
-    query_cols = lax.all_to_all(query, "ctx", split_axis=0, concat_axis=0, tiled=True)
-    cot_all = lax.all_gather(cotangent, "ctx", axis=0, tiled=True).reshape(blocks, lane, features)
     vmem = pl.BlockSpec(memory_space=pltpu.VMEM)
+    anywhere = pl.BlockSpec(memory_space=pl.ANY)
+    dma = pltpu.SemaphoreType.DMA
+    tile = pltpu.VMEM(tile_shape, jnp.bfloat16)
     qgrad, mgrad, filter_grad = pl.pallas_call(
-        channel_kernel,
-        in_specs=[vmem] * 5,
-        out_specs=[vmem] * 3,
+        slice_kernel,
+        in_specs=[anywhere] * 3 + [vmem] * 2,
+        out_specs=[anywhere] * 2 + [vmem],
         out_shape=[
             jax.ShapeDtypeStruct(tile_shape, jnp.bfloat16),
             jax.ShapeDtypeStruct(tile_shape, jnp.bfloat16),
             jax.ShapeDtypeStruct(filters.shape, jnp.float32),
         ],
         scratch_shapes=[
-            pltpu.VMEM(tile_shape, jnp.bfloat16),
+            tile,
+            tile,
+            pltpu.VMEM((blocks, lane, features), jnp.bfloat16),
+            tile,
+            tile,
+            tile,
             pltpu.VMEM(tile_shape, jnp.float32),
             pltpu.VMEM((blocks, 2 * lane, seq_len), jnp.bfloat16),
             pltpu.VMEM((filters.shape[0], seq_len + lane), jnp.float32),
+            dma((4, blocks)),
+            dma((blocks,)),
+            dma((blocks,)),
+            dma((blocks,)),
+            dma((blocks,)),
+            dma((blocks,)),
+            dma((blocks,)),
+            dma((blocks,)),
+            dma((2, blocks)),
+            dma((2, blocks)),
+            dma((6,)),
         ],
-        compiler_params=pltpu.CompilerParams(vmem_limit_bytes=52 * 1024 * 1024),
+        compiler_params=pltpu.CompilerParams(
+            collective_id=0, has_side_effects=True, vmem_limit_bytes=52 * 1024 * 1024
+        ),
         cost_estimate=pl.CostEstimate(
             flops=8 << 30, bytes_accessed=16 << 20, transcendentals=0
         ),
-    )(mixed_cols, query_cols, cot_all, out_weight, filters)
-    qgrad = lax.all_to_all(qgrad, "ctx", split_axis=0, concat_axis=0, tiled=True)
-    mgrad = lax.all_to_all(mgrad, "ctx", split_axis=0, concat_axis=0, tiled=True)
+    )(mixed, query, cotangent, out_weight, filters)
     return (*finish(qgrad, mgrad, key_proj, value_proj), filter_grad)
 
 

time: 221 us -> 162 us (0.73)
  Pallas kernels: 29.1 us -> 153 us
  blocking collectives: 114 us -> 0 us
  waiting for transfers between devices: 50.9 us -> 0 us
  between operations: 14.1 us -> 0.68 us
  starting transfers between devices: 7.47 us -> 0 us
  local copies, waits for them, and re-layouts: 3.74 us -> 6.56 us
    pallas_call x1, Pallas kernels: 25.9 us -> 150 us  [direct_device(): pl.pallas_call(slice_kernel, in_specs=[anywhere] * 3 + [vmem] * 2, out_sp...]
    all_to_all x3 -> x0, blocking collectives: 114 us -> none  [the longest x1 56.4 us: direct_device(): lax.all_to_all(mixed, 'ctx', split_axis=0, concat_axis=0, tiled=True)]
    all_to_all x1 -> x0, waiting for transfers between devices: 35.4 us -> none  [direct_device(): lax.all_to_all(query, 'ctx', split_axis=0, concat_axis=0, tiled=True)]
    all_gather x1 -> x0, waiting for transfers between devices: 14.8 us -> none  [direct_device(): lax.all_gather(cotangent, 'ctx', axis=0, tiled=True)]
    all_to_all x1 -> x0, starting transfers between devices: 7.44 us -> none  [direct_device(): lax.all_to_all(query, 'ctx', split_axis=0, concat_axis=0, tiled=True)]
  transfers between devices with their start and end apart: 2 -> 0, of which waited for: 2 -> 0; matrix products, arithmetic and copies ran while one was open for 2% -> 0% of each run, Pallas kernels for 0% -> 0%
where the time goes in v2:
time: 162 us
  Pallas kernels  153 us (94%)
  local copies, waits for them, and re-layouts  6.56 us (4%)
    pallas_call x1, Pallas kernels, direct_device(): pl.pallas_call(slice_kernel, in_specs=[anywhere] * 3 + [vmem] * 2, out_sp...  150 us

profile of v2, /device:TPU:0, one launch (start us, length us, event | category | flops | bytes accessed | tf_op | source)
XLA Modules:
  0.0 161.5 jit_solution(4613721702595236423)
XLA Ops:
  0.6 0.0 copy-start
  0.6 0.0 copy-start.1
  0.7 2.4 %copy.11 = bf16[4096,128]{1,0:T(8,128)(2,1)} copy(bf16[4096,128]{0,1:T(8,128)(2,1)} %bitcast.9) | data formatting | bytes 2097152 | tf_op jit(solution)/shard_map/transpose | solution.py:497
  3.1 0.0 copy-done
  3.1 0.0 copy-done.1
  3.1 0.0 copy-start.3
  3.1 0.0 copy-start.4
  3.1 1.2 multiply_convert_fusion
  4.3 2.3 %copy.10 = bf16[4096,128]{1,0:T(8,128)(2,1)} copy(bf16[4096,128]{0,1:T(8,128)(2,1)} %bitcast.8) | data formatting | bytes 2097152 | tf_op jit(solution)/shard_map/transpose | solution.py:496
  6.6 0.0 copy-done.3
  6.6 0.0 copy-done.4
  6.6 149.9 %shard_map.93 = (bf16[16,256,128]{2,1,0:T(8,128)(2,1)S(1)}, bf16[16,256,128]{2,1,0:T(8,128)(2,1)}, f32[16,2048]{1,0:T(8,128)S(1)}) custom-call(bf16[16,256,128]{2,1,0:T(8,128)(2,1)} %bitcast.11, bf16[16,256,128]{2,1,0:T(8,128)(2,1)} %bitcast.10, bf16[128,2048]{1,0:T(8,128)(2,1)S(1)} %copy-done.3, bf16[256,2048]{1,0:T(8,128)(2,1)} %weight_ref.1, ...), custom_call_target="tpu_custom_call" | custom-call | flops 8589934592 | bytes 16777216 | tf_op jit(solution)/shard_map/pallas_call | solution.py:502
  156.5 0.0 copy-start.2
  156.5 1.2 copy-done.2
  157.7 3.2 %shard_map.94 = (f32[128,4096]{1,0:T(8,128)}, f32[128,4096]{1,0:T(8,128)}, f32[128,4096]{1,0:T(8,128)}) custom-call(bf16[4096,128]{1,0:T(8,128)(2,1)S(1)} %bitcast.6, bf16[4096,128]{1,0:T(8,128)(2,1)S(1)} %bitcast.7, bf16[128,4096]{1,0:T(8,128)(2,1)S(1)} %copy-done.1, bf16[128,4096]{1,0:T(8,128)(2,1)S(1)} %copy-done), custom_call_target="tpu_custom_call" | custom-call | flops 1048576 | bytes 10485760 | tf_op jit(solution)/shard_map/pallas_call | solution.py:479
  160.9 0.7 copy.13
Async XLA Ops:
  0.6 2.4 %copy-start = (bf16[128,4096]{1,0:T(8,128)(2,1)S(1)}, bf16[128,4096]{1,0:T(8,128)(2,1)}, u32[]{:S(2)}) copy-start(bf16[128,4096]{1,0:T(8,128)(2,1)} %value_ref.1) | copy-start | bytes 3145732
  0.6 2.4 %copy-start.1 = (bf16[128,4096]{1,0:T(8,128)(2,1)S(1)}, bf16[128,4096]{1,0:T(8,128)(2,1)}, u32[]{:S(2)}) copy-start(bf16[128,4096]{1,0:T(8,128)(2,1)} %key_ref.1) | copy-start | bytes 3145732
  3.1 3.5 %copy-start.3 = (bf16[128,2048]{1,0:T(8,128)(2,1)S(1)}, bf16[128,2048]{1,0:T(8,128)(2,1)}, u32[]{:S(2)}) copy-start(bf16[128,2048]{1,0:T(8,128)(2,1)} %cot_ref.1) | copy-start | bytes 1572868
  3.1 3.5 %copy-start.4 = (f32[16,2048]{1,0:T(8,128)S(1)}, f32[16,2048]{1,0:T(8,128)}, u32[]{:S(2)}) copy-start(f32[16,2048]{1,0:T(8,128)} %filt_ref.1) | copy-start | bytes 393220
  156.5 1.2 copy-start.2

commit v3 on v2

--- a/solution.py
+++ b/solution.py
@@ -223,13 +223,6 @@
     store_pairs(conv_ref, rows, jnp.dot(left, right, preferred_element_type=jnp.float32))
 
 
-def query_group(group, conv_ref, grad_ref, out_ref):
-    rows = group_rows(group)
-    out_ref[:, rows, :] = (
-        conv_ref[:, rows, :] * grad_ref[:, rows, :].astype(jnp.float32)
-    ).astype(out_ref.dtype)
-
-
 def gated_of(rows, query_ref, grad_ref):
     return (
         query_ref[:, rows, :].astype(jnp.float32) * grad_ref[:, rows, :].astype(jnp.float32)
@@ -281,8 +274,9 @@
 
 
 def slice_kernel(
-    mixed_ref, query_ref, cot_ref, weight_ref, filt_ref,
+    query_hbm, key_hbm, value_hbm, cot_ref, weight_hbm, filt_ref,
     qback_ref, mback_ref, fgrad_ref,
+    query_rows, key_rows, value_rows, weight_ref, mixed_ref, query_ref,
     mixed_in, query_in, cot_in, qgrad_ref, mgrad_ref, grad_ref, conv_ref, toep_ref, lag_ref,
     cot_send, cot_recv, mixed_send, mixed_recv, query_send, query_recv,
     qback_send, qback_recv, mback_send, mback_recv, local_sem,
@@ -294,6 +288,20 @@
 
     def peer_of(step):
         return (me + step) % blocks
+
+    loads = [
+        pltpu.make_async_copy(src, dst, local_sem.at[6 + index])
+        for index, (src, dst) in enumerate(
+            [
+                (key_hbm, key_rows),
+                (value_hbm, value_rows),
+                (query_hbm, query_rows),
+                (weight_hbm, weight_ref),
+            ]
+        )
+    ]
+    for load in loads:
+        load.start()
 
     barrier = pltpu.get_barrier_semaphore()
 
@@ -403,44 +411,103 @@
         for half in range(halves)
     ]
 
+    def columns(dest):
+        own = mixed_in.shape[1]
+        return pl.ds(pl.multiple_of(dest * own, own), own)
+
+    def grad_pair(block):
+        other = block + 1 - 2 * place_core
+        arrived(other)
+        grad_block(block // 2, weight_ref, cot_in, grad_ref)
+
+    def finish_block(dest):
+        qgrad_ref[dest] = (
+            conv_ref[dest] * grad_ref[dest].astype(jnp.float32)
+        ).astype(jnp.bfloat16)
+
+    def send_block(dest):
+        finish_block(dest)
+        remote(
+            qgrad_ref.at[dest], qback_ref.at[me], qback_send.at[dest], qback_recv.at[me], dest
+        ).start()
+
+    def send_pair(block):
+        send_block(block)
+        send_block(block + 1 - 2 * place_core)
+
+    def both_z(hop, base, act):
+        @pl.when(place_z >= hop)
+        def _():
+            act(base - 4 * hop)
+
+        @pl.when(place_z + hop <= 3)
+        def _():
+            act(base + 4 * hop)
+
+    def grad_and_send(block):
+        grad_pair(block)
+        send_pair(block)
+
     forward(cot_ref, me, "udyc", begin)
     own_cot = pltpu.make_async_copy(cot_ref, cot_in.at[me], local_sem.at[3])
     own_cot.start()
-    start_all(*mixed_trip)
+    loads[0].wait()
+    loads[1].wait()
+
+    def make_mixed(dest):
+        at = columns(dest)
+        product = key_rows[:, at].astype(jnp.float32) * value_rows[:, at].astype(jnp.float32)
+        mixed_ref[dest] = product.T.astype(jnp.bfloat16)
+
+    @pl.loop(1, blocks)
+    def _(step):
+        peer = peer_of(step)
+        make_mixed(peer)
+        remote(
+            mixed_ref.at[peer], mixed_in.at[me], mixed_send.at[peer], mixed_recv.at[me], peer
+        ).start()
+
+    make_mixed(me)
+    pltpu.make_async_copy(mixed_ref.at[me, every], mixed_in.at[me, every], local_sem.at[0]).start()
+    loads[2].wait()
+
+    @pl.loop(0, blocks)
+    def _(dest):
+        query_ref[dest] = query_rows[:, columns(dest)].astype(jnp.float32).T.astype(jnp.bfloat16)
 
     @pl.loop(0, blocks)
     def _(group):
         toep_ref[group] = toeplitz(filt_ref[pl.ds(group, 1), :])
 
+    own_cot.wait()
+    loads[3].wait()
     relay_z(1, begin, True)
     relay_y(0, begin, True)
+    grad_pair(me)
     relay_z(2, begin, True)
     relay_y(1, begin, True)
     start_all(*query_trip)
+    both_z(1, me, grad_pair)
+    grad_pair(y_peer)
     relay_z(3, begin, True)
+    relay_y(2, begin, True)
     wait_arrivals(*mixed_trip)
 
     @pl.loop(0, blocks)
     def _(group):
         conv_group(group, mixed_in, toep_ref, conv_ref)
 
-    relay_y(2, begin, True)
+    finish_block(me)
+    pltpu.make_async_copy(qgrad_ref.at[me, every], qback_ref.at[me, every], local_sem.at[2]).start()
+    send_block(core_peer)
+    both_z(1, me, send_pair)
+    send_pair(y_peer)
     relay_y(3, begin, True)
-    own_cot.wait()
-
-    @pl.loop(0, blocks // 2)
-    def _(pair):
-        arrived(2 * pair + 1 - place_core)
-
-    @pl.loop(0, blocks // 2)
-    def _(pair):
-        grad_block(pair, weight_ref, cot_in, grad_ref)
-
-    @pl.loop(0, blocks)
-    def _(group):
-        query_group(group, conv_ref, grad_ref, qgrad_ref)
-
-    start_all(*qback_trip)
+    both_z(2, me, grad_and_send)
+    both_z(1, y_peer, grad_and_send)
+    both_z(3, me, grad_and_send)
+    both_z(2, y_peer, grad_and_send)
+    both_z(3, y_peer, grad_and_send)
     wait_arrivals(*query_trip)
     for half in range(halves):
         @pl.loop(half * blocks // halves, (half + 1) * blocks // halves)
@@ -493,15 +560,14 @@
     features = cotangent.shape[1]
     seq_len = filters.shape[1]
     tile_shape = (blocks, own, lane)
-    mixed = rounded_product(key_proj, value_proj).T.reshape(tile_shape)
-    query = query_proj.T.reshape(tile_shape)
     vmem = pl.BlockSpec(memory_space=pltpu.VMEM)
     anywhere = pl.BlockSpec(memory_space=pl.ANY)
     dma = pltpu.SemaphoreType.DMA
     tile = pltpu.VMEM(tile_shape, jnp.bfloat16)
+    rows = pltpu.VMEM(query_proj.shape, jnp.bfloat16)
     qgrad, mgrad, filter_grad = pl.pallas_call(
         slice_kernel,
-        in_specs=[anywhere] * 3 + [vmem] * 2,
+        in_specs=[anywhere] * 5 + [vmem],
         out_specs=[anywhere] * 2 + [vmem],
         out_shape=[
             jax.ShapeDtypeStruct(tile_shape, jnp.bfloat16),
@@ -509,6 +575,12 @@
             jax.ShapeDtypeStruct(filters.shape, jnp.float32),
         ],
         scratch_shapes=[
+            rows,
+            rows,
+            rows,
+            pltpu.VMEM(out_weight.shape, jnp.bfloat16),
+            tile,
+            tile,
             tile,
             tile,
             pltpu.VMEM((blocks, lane, features), jnp.bfloat16),
@@ -528,7 +600,7 @@
             dma((blocks,)),
             dma((2, blocks)),
             dma((2, blocks)),
-            dma((6,)),
+            dma((10,)),
         ],
         compiler_params=pltpu.CompilerParams(
             collective_id=0, has_side_effects=True, vmem_limit_bytes=52 * 1024 * 1024
@@ -536,7 +608,7 @@
         cost_estimate=pl.CostEstimate(
             flops=8 << 30, bytes_accessed=16 << 20, transcendentals=0
         ),
-    )(mixed, query, cotangent, out_weight, filters)
+    )(query_proj, key_proj, value_proj, cotangent, out_weight, filters)
     return (*finish(qgrad, mgrad, key_proj, value_proj), filter_grad)
 
 

time: 162 us -> 147 us (0.907)
  Pallas kernels: 153 us -> 142 us
  local copies, waits for them, and re-layouts: 6.56 us -> 3.97 us
    pallas_call x1, Pallas kernels: 150 us -> 139 us  [direct_device(): pl.pallas_call(slice_kernel, in_specs=[anywhere] * 5 + [vmem], out_specs=...]
    transpose x2 -> x0, local copies, waits for them, and re-layouts: 4.67 us -> none  [the longest x1 2.41 us: direct_device(): query = query_proj.T.reshape(tile_shape)]
    unnamed x11, local copies, waits for them, and re-layouts: 1.89 us -> 3.97 us
where the time goes in v3:
time: 147 us; the launch traced here: 146 us
  Pallas kernels  142 us (97%)
  local copies, waits for them, and re-layouts  3.97 us (3%)
    pallas_call x1, Pallas kernels, direct_device(): pl.pallas_call(slice_kernel, in_specs=[anywhere] * 5 + [vmem], out_specs=...  139 us
    unnamed x11, local copies, waits for them, and re-layouts  3.97 us
    pallas_call x1, Pallas kernels, finish(): pl.pallas_call(final_kernel, grid=(4,), in_specs=[pl.BlockSpec((wide, lan...  3.16 us

profile of v3, /device:TPU:0, one launch (start us, length us, event | category | flops | bytes accessed | tf_op | source)
XLA Modules:
  0.0 146.3 jit_solution(1204834990092959945)
XLA Ops:
  0.6 0.0 copy-start.1
  0.6 0.0 copy-start
  0.7 0.0 copy-start.3
  0.7 1.2 copy-done.3
  1.8 0.0 copy-start.4
  1.8 0.9 copy-done.4
  2.7 138.5 %shard_map.93 = (bf16[16,256,128]{2,1,0:T(8,128)(2,1)S(1)}, bf16[16,256,128]{2,1,0:T(8,128)(2,1)}, f32[16,2048]{1,0:T(8,128)S(1)}) custom-call(bf16[128,4096]{1,0:T(8,128)(2,1)} %query_hbm.1, bf16[128,4096]{1,0:T(8,128)(2,1)} %key_ref.1, bf16[128,4096]{1,0:T(8,128)(2,1)} %value_ref.1, bf16[128,2048]{1,0:T(8,128)(2,1)S(1)} %copy-done.3, ...), custom_call_target="tpu_custom_call" | custom-call | flops 8589934592 | bytes 16777216 | tf_op jit(solution)/shard_map/pallas_call | solution.py:568
  141.3 0.0 copy-done.1
  141.3 0.0 copy-done
  141.3 0.0 copy-start.2
  141.3 1.2 copy-done.2
  142.5 3.2 %shard_map.94 = (f32[128,4096]{1,0:T(8,128)}, f32[128,4096]{1,0:T(8,128)}, f32[128,4096]{1,0:T(8,128)}) custom-call(bf16[4096,128]{1,0:T(8,128)(2,1)S(1)} %bitcast.2, bf16[4096,128]{1,0:T(8,128)(2,1)S(1)} %bitcast.3, bf16[128,4096]{1,0:T(8,128)(2,1)S(1)} %copy-done, bf16[128,4096]{1,0:T(8,128)(2,1)S(1)} %copy-done.1), custom_call_target="tpu_custom_call" | custom-call | flops 1048576 | bytes 10485760 | tf_op jit(solution)/shard_map/pallas_call | solution.py:546
  145.7 0.7 copy.11
Async XLA Ops:
  0.6 140.6 %copy-start.1 = (bf16[128,4096]{1,0:T(8,128)(2,1)S(1)}, bf16[128,4096]{1,0:T(8,128)(2,1)}, u32[]{:S(2)}) copy-start(bf16[128,4096]{1,0:T(8,128)(2,1)} %value_ref.1) | copy-start | bytes 3145732
  0.6 140.6 %copy-start = (bf16[128,4096]{1,0:T(8,128)(2,1)S(1)}, bf16[128,4096]{1,0:T(8,128)(2,1)}, u32[]{:S(2)}) copy-start(bf16[128,4096]{1,0:T(8,128)(2,1)} %key_ref.1) | copy-start | bytes 3145732
  0.7 1.2 copy-start.3
  1.8 0.9 copy-start.4
  141.3 1.2 copy-start.2
